TPU v7x, 32 devices: a whole 2x2x4 slice. The times are simulated.
32 devices in a mesh: dp: 4 (over z), tensor: 8 (over y, x, core).
Axes of the slice: x: 2, y: 2, z: 4, core: 2. Of those that a mesh axis runs over, the one named last changes fastest.
Arguments:
- queries: bfloat16 [4096, 2048], P(('dp', 'tensor'))
- key_rows: bfloat16 [4096, 1024], P(('dp', 'tensor'))
- value_rows: bfloat16 [4096, 1024], P(('dp', 'tensor')), may hold values from -6 to 6
- out_grad: bfloat16 [4096, 2048], P(('dp', 'tensor')), may hold values from -6 to 6
Outputs:
- attended: bfloat16 [4096, 2048], P(('dp', 'tensor'))
- grad_queries: bfloat16 [4096, 2048], P(('dp', 'tensor'))
- grad_keys: bfloat16 [4096, 1024], P(('dp', 'tensor'))
- grad_values: bfloat16 [4096, 1024], P(('dp', 'tensor'))
All inputs are finite; a program needn't handle non-finite values.
Results may differ from a plain program's by a relative error of at most 0.0075.
Values may be sent and summed in bfloat16 or wider, within the bound.
A program may use at most 64 MiB of HBM per device.

v0:
```python
import jax
import jax.numpy as jnp
from jax import lax
from jax.sharding import PartitionSpec as P

HEAD_DIM = 128
WINDOW = 1024
QUERY_SCALE = 168


masked_score = -1e30


def from_behind(value, axis, by):
    peers = lax.axis_size(axis)
    pairs = [(i, i + by) for i in range(peers) if 0 <= i + by < peers]
    return lax.ppermute(value, axis, pairs)


def local(queries, key_rows, value_rows, out_grad):
    row_count = queries.shape[0]
    group_count = key_rows.shape[1] // HEAD_DIM
    repeat_count = queries.shape[1] // key_rows.shape[1]
    reach_count = WINDOW // row_count
    score_scale = QUERY_SCALE ** (-0.5)
    near_keys = key_rows
    near_values = value_rows
    for distance in range(1, reach_count + 1):
        prior_keys, prior_values = from_behind((key_rows, value_rows), ("dp", "tensor"), distance)
        near_keys = jnp.concatenate([prior_keys, near_keys], axis=0)
        near_values = jnp.concatenate([prior_values, near_values], axis=0)
    span_rows = near_keys.shape[0]
    first_row = lax.axis_index(("dp", "tensor")) * row_count
    query_pos = first_row + lax.broadcasted_iota(jnp.int32, (row_count, span_rows), 0)
    key_pos = first_row - WINDOW + lax.broadcasted_iota(jnp.int32, (row_count, span_rows), 1)
    allowed = (key_pos <= query_pos) & (key_pos > query_pos - WINDOW) & (key_pos >= 0)
    group_width = repeat_count * HEAD_DIM

    def group_step(group_index, state):
        attended, grad_queries, key_terms, value_terms = state
        query_start = group_index * group_width
        key_start = group_index * HEAD_DIM
        query_group = lax.dynamic_slice_in_dim(queries, query_start, group_width, 1).reshape(
            row_count, repeat_count, HEAD_DIM
        )
        grad_group = lax.dynamic_slice_in_dim(out_grad, query_start, group_width, 1).reshape(
            row_count, repeat_count, HEAD_DIM
        )
        key_group = lax.dynamic_slice_in_dim(near_keys, key_start, HEAD_DIM, 1)
        value_group = lax.dynamic_slice_in_dim(near_values, key_start, HEAD_DIM, 1)
        scores = score_scale * jnp.einsum(
            "ird,jd->rij", query_group, key_group, preferred_element_type=jnp.float32
        )
        scores = jnp.where(allowed[None], scores, masked_score)
        peak = jnp.max(scores, axis=-1, keepdims=True)
        expo = jnp.exp(scores - peak)
        probs = expo / jnp.sum(expo, axis=-1, keepdims=True)
        probs_low = probs.astype(jnp.bfloat16)
        out_full = jnp.einsum(
            "rij,jd->ird", probs_low, value_group, preferred_element_type=jnp.float32
        )
        grad_probs = jnp.einsum(
            "ird,jd->rij", grad_group, value_group, preferred_element_type=jnp.float32
        )
        delta = jnp.sum(grad_group.astype(jnp.float32) * out_full, axis=-1).T
        grad_scores = (score_scale * probs * (grad_probs - delta[:, :, None])).astype(jnp.bfloat16)
        grad_query = jnp.einsum(
            "rij,jd->ird", grad_scores, key_group, preferred_element_type=jnp.float32
        )
        key_term = jnp.einsum(
            "rij,ird->jd", grad_scores, query_group, preferred_element_type=jnp.float32
        ).astype(jnp.bfloat16)
        value_term = jnp.einsum(
            "rij,ird->jd", probs_low, grad_group, preferred_element_type=jnp.float32
        ).astype(jnp.bfloat16)
        attended = lax.dynamic_update_slice_in_dim(
            attended, out_full.astype(jnp.bfloat16).reshape(row_count, group_width), query_start, 1
        )
        grad_queries = lax.dynamic_update_slice_in_dim(
            grad_queries,
            grad_query.astype(jnp.bfloat16).reshape(row_count, group_width),
            query_start,
            1,
        )
        key_terms = lax.dynamic_update_slice_in_dim(key_terms, key_term, key_start, 1)
        value_terms = lax.dynamic_update_slice_in_dim(value_terms, value_term, key_start, 1)
        return (attended, grad_queries, key_terms, value_terms)

    start_state = (
        jnp.zeros(queries.shape, jnp.bfloat16),
        jnp.zeros(queries.shape, jnp.bfloat16),
        jnp.zeros(near_keys.shape, jnp.bfloat16),
        jnp.zeros(near_values.shape, jnp.bfloat16),
    )
    attended, grad_queries, key_terms, value_terms = lax.fori_loop(
        0, group_count, group_step, start_state
    )
    own_start = span_rows - row_count
    total_keys = key_terms[own_start:].astype(jnp.float32)
    total_values = value_terms[own_start:].astype(jnp.float32)
    for distance in range(1, reach_count + 1):
        begin_row = (reach_count - distance) * row_count
        later_keys, later_values = from_behind(
            (
                key_terms[begin_row : begin_row + row_count],
                value_terms[begin_row : begin_row + row_count],
            ),
            ("dp", "tensor"),
            -distance,
        )
        total_keys = total_keys + later_keys.astype(jnp.float32)
        total_values = total_values + later_values.astype(jnp.float32)
    return (
        attended,
        grad_queries,
        total_keys.astype(jnp.bfloat16),
        total_values.astype(jnp.bfloat16),
    )


def solution(mesh):
    in_specs = (
        P(("dp", "tensor"), None),
        P(("dp", "tensor"), None),
        P(("dp", "tensor"), None),
        P(("dp", "tensor"), None),
    )
    out_specs = (
        P(("dp", "tensor"), None),
        P(("dp", "tensor"), None),
        P(("dp", "tensor"), None),
        P(("dp", "tensor"), None),
    )
    return jax.shard_map(local, mesh=mesh, in_specs=in_specs, out_specs=out_specs, check_vma=False)
```

profile of v0, /device:TPU:16, one launch (start us, length us, event | category | flops | bytes accessed | tf_op | source)
XLA Modules:
  0.0 308.1 jit_solution(4305307932729928119)
XLA Ops:
  3.7 3.4 %collective-permute-start.6 = (bf16[128,1024]{0,1:T(8,128)(2,1)S(1)}, bf16[128,1024]{0,1:T(8,128)(2,1)S(1)}, u32[]{:S(2)}, u32[]{:S(2)}) collective-permute-start(bf16[128,1024]{0,1:T(8,128)(2,1)S(1)} %copy.34), channel_id=1, source_target_pairs={{0,2},{1,3},{2,4},{3,5},{4,6},{5,7},{6,8},{7,9},{8,10},{9,11},{10,... | collective-permute-start | bytes 786440 | tf_op jit(solution)/shard_map/ppermute | solution.py:17
  7.1 4.4 %collective-permute-start.10 = (bf16[128,1024]{1,0:T(8,128)(2,1)}, bf16[128,1024]{1,0:T(8,128)(2,1)S(1)}, u32[]{:S(2)}, u32[]{:S(2)}) collective-permute-start(bf16[128,1024]{1,0:T(8,128)(2,1)} %param.7), channel_id=1, source_target_pairs={{0,6},{1,7},{2,8},{3,9},{4,10},{5,11},{6,12},{7,13},{8,14},{9,15},... | collective-permute-start | bytes 786440 | tf_op jit(solution)/shard_map/ppermute | solution.py:17
  11.5 2.9 collective-permute-start.9
  16.4 8.6 %collective-permute-done.8 = bf16[128,1024]{1,0:T(8,128)(2,1)S(1)} collective-permute-done((bf16[128,1024]{1,0:T(8,128)(2,1)}, bf16[128,1024]{1,0:T(8,128)(2,1)S(1)}, u32[]{:S(2)}, u32[]{:S(2)}) %collective-permute-start.8) | collective-permute-done | bytes 262176 | tf_op jit(solution)/shard_map/ppermute | solution.py:17
  25.0 8.4 %collective-permute-start.11 = (bf16[128,1024]{1,0:T(8,128)(2,1)}, bf16[128,1024]{1,0:T(8,128)(2,1)S(1)}, u32[]{:S(2)}, u32[]{:S(2)}) collective-permute-start(bf16[128,1024]{1,0:T(8,128)(2,1)} %param.7), channel_id=1, source_target_pairs={{0,5},{1,6},{2,7},{3,8},{4,9},{5,10},{6,11},{7,12},{8,13},{9,14},{... | collective-permute-start | bytes 786440 | tf_op jit(solution)/shard_map/ppermute | solution.py:17
  33.5 2.2 collective-permute-start.12
  35.7 4.4 %collective-permute-start.13 = (bf16[128,1024]{1,0:T(8,128)(2,1)}, bf16[128,1024]{1,0:T(8,128)(2,1)S(1)}, u32[]{:S(2)}, u32[]{:S(2)}) collective-permute-start(bf16[128,1024]{1,0:T(8,128)(2,1)} %param.7), channel_id=1, source_target_pairs={{0,3},{1,4},{2,5},{3,6},{4,7},{5,8},{6,9},{7,10},{8,11},{9,12},{10... | collective-permute-start | bytes 786440 | tf_op jit(solution)/shard_map/ppermute | solution.py:17
  40.1 7.1 %collective-permute-start.14 = (bf16[128,1024]{1,0:T(8,128)(2,1)}, bf16[128,1024]{1,0:T(8,128)(2,1)S(1)}, u32[]{:S(2)}, u32[]{:S(2)}) collective-permute-start(bf16[128,1024]{1,0:T(8,128)(2,1)} %param.7), channel_id=1, source_target_pairs={{0,2},{1,3},{2,4},{3,5},{4,6},{5,7},{6,8},{7,9},{8,10},{9,11},{10,... | collective-permute-start | bytes 786440 | tf_op jit(solution)/shard_map/ppermute | solution.py:17
  49.6 7.0 %collective-permute-start.2 = (bf16[128,1024]{0,1:T(8,128)(2,1)S(1)}, bf16[128,1024]{0,1:T(8,128)(2,1)S(1)}, u32[]{:S(2)}, u32[]{:S(2)}) collective-permute-start(bf16[128,1024]{0,1:T(8,128)(2,1)S(1)} %copy.34), channel_id=1, source_target_pairs={{0,6},{1,7},{2,8},{3,9},{4,10},{5,11},{6,12},{7,13},{8,14},{9,15},... | collective-permute-start | bytes 786440 | tf_op jit(solution)/shard_map/ppermute | solution.py:17
  56.6 3.4 %collective-permute-done.14 = bf16[128,1024]{1,0:T(8,128)(2,1)S(1)} collective-permute-done((bf16[128,1024]{1,0:T(8,128)(2,1)}, bf16[128,1024]{1,0:T(8,128)(2,1)S(1)}, u32[]{:S(2)}, u32[]{:S(2)}) %collective-permute-start.14) | collective-permute-done | bytes 262176 | tf_op jit(solution)/shard_map/ppermute | solution.py:17
  60.0 3.5 %collective-permute-start = (bf16[128,1024]{0,1:T(8,128)(2,1)S(1)}, bf16[128,1024]{0,1:T(8,128)(2,1)S(1)}, u32[]{:S(2)}, u32[]{:S(2)}) collective-permute-start(bf16[128,1024]{0,1:T(8,128)(2,1)S(1)} %copy.34), channel_id=1, source_target_pairs={{0,8},{1,9},{2,10},{3,11},{4,12},{5,13},{6,14},{7,15},{8,16},{9,17... | collective-permute-start | bytes 786440 | tf_op jit(solution)/shard_map/ppermute | solution.py:17
  63.5 2.7 collective-permute-start.1
  66.3 4.6 %collective-permute-done = bf16[128,1024]{0,1:T(8,128)(2,1)S(1)} collective-permute-done((bf16[128,1024]{0,1:T(8,128)(2,1)S(1)}, bf16[128,1024]{0,1:T(8,128)(2,1)S(1)}, u32[]{:S(2)}, u32[]{:S(2)}) %collective-permute-start) | collective-permute-done | bytes 262176 | tf_op jit(solution)/shard_map/ppermute | solution.py:17
  72.9 5.7 %collective-permute-start.4 = (bf16[128,1024]{0,1:T(8,128)(2,1)S(1)}, bf16[128,1024]{0,1:T(8,128)(2,1)S(1)}, u32[]{:S(2)}, u32[]{:S(2)}) collective-permute-start(bf16[128,1024]{0,1:T(8,128)(2,1)S(1)} %copy.34), channel_id=1, source_target_pairs={{0,4},{1,5},{2,6},{3,7},{4,8},{5,9},{6,10},{7,11},{8,12},{9,13},{1... | collective-permute-start | bytes 786440 | tf_op jit(solution)/shard_map/ppermute | solution.py:17
  78.7 4.1 %collective-permute-start.5 = (bf16[128,1024]{0,1:T(8,128)(2,1)S(1)}, bf16[128,1024]{0,1:T(8,128)(2,1)S(1)}, u32[]{:S(2)}, u32[]{:S(2)}) collective-permute-start(bf16[128,1024]{0,1:T(8,128)(2,1)S(1)} %copy.34), channel_id=1, source_target_pairs={{0,3},{1,4},{2,5},{3,6},{4,7},{5,8},{6,9},{7,10},{8,11},{9,12},{10... | collective-permute-start | bytes 786440 | tf_op jit(solution)/shard_map/ppermute | solution.py:17
  84.9 5.3 %collective-permute-done.5 = bf16[128,1024]{0,1:T(8,128)(2,1)S(1)} collective-permute-done((bf16[128,1024]{0,1:T(8,128)(2,1)S(1)}, bf16[128,1024]{0,1:T(8,128)(2,1)S(1)}, u32[]{:S(2)}, u32[]{:S(2)}) %collective-permute-start.5) | collective-permute-done | bytes 262176 | tf_op jit(solution)/shard_map/ppermute | solution.py:17
  95.1 115.4 %while.20 = (s32[]{:T(128)}, bf16[128,2048]{1,0:T(8,128)(2,1)}, bf16[128,2048]{1,0:T(8,128)(2,1)}, bf16[1152,1024]{1,0:T(8,128)(2,1)}, bf16[1152,1024]{1,0:T(8,1...) while((s32[]{:T(128)}, bf16[128,2048]{1,0:T(8,128)(2,1)}, ...), condition=%wide.region_4.5_spmd.clone, body=%wide.region_0.4_spmd.clone.sunk | while | flops 610635392 | bytes 8731565 | solution.py:95
  97.9 2.6 fusion.93
  107.4 2.1 fusion.96
  112.3 2.6 fusion.93
  121.8 2.1 fusion.96
  126.7 2.6 fusion.93
  136.3 2.1 fusion.96
  141.2 2.6 fusion.93
  155.6 2.6 fusion.93
  165.2 2.1 fusion.96
  170.1 2.6 fusion.93
  179.6 2.1 fusion.96
  184.5 2.6 fusion.93
  194.0 2.1 fusion.96
  198.9 2.6 fusion.93
  210.8 7.1 %collective-permute-start.24 = (bf16[128,1024]{1,0:T(8,128)(2,1)S(1)}, bf16[128,1024]{1,0:T(8,128)(2,1)S(1)}, u32[]{:S(2)}, u32[]{:S(2)}) collective-permute-start(bf16[128,1024]{1,0:T(8,128)(2,1)S(1)} %get-tuple-element.279), channel_id=1, source_target_pairs={{1,0},{2,1},{3,2},{4,3},{5,4},{6,5},{7,6},{8,7},{9,8},{10,9},{11,1... | collective-permute-start | bytes 786440 | tf_op jit(solution)/shard_map/ppermute | solution.py:17
  217.8 2.3 collective-permute-start.30
  220.1 3.4 %collective-permute-start.29 = (bf16[128,1024]{1,0:T(8,128)(2,1)S(1)}, bf16[128,1024]{1,0:T(8,128)(2,1)S(1)}, u32[]{:S(2)}, u32[]{:S(2)}) collective-permute-start(bf16[128,1024]{1,0:T(8,128)(2,1)S(1)} %get-tuple-element.281), channel_id=1, source_target_pairs={{6,0},{7,1},{8,2},{9,3},{10,4},{11,5},{12,6},{13,7},{14,8},{15,9},... | collective-permute-start | bytes 786440 | tf_op jit(solution)/shard_map/ppermute | solution.py:17
  229.5 3.4 %collective-permute-start.25 = (bf16[128,1024]{1,0:T(8,128)(2,1)S(1)}, bf16[128,1024]{1,0:T(8,128)(2,1)S(1)}, u32[]{:S(2)}, u32[]{:S(2)}) collective-permute-start(bf16[128,1024]{1,0:T(8,128)(2,1)S(1)} %get-tuple-element.285), channel_id=1, source_target_pairs={{2,0},{3,1},{4,2},{5,3},{6,4},{7,5},{8,6},{9,7},{10,8},{11,9},{12,... | collective-permute-start | bytes 786440 | tf_op jit(solution)/shard_map/ppermute | solution.py:17
  234.8 6.4 %collective-permute-done.28 = bf16[128,1024]{1,0:T(8,128)(2,1)S(1)} collective-permute-done((bf16[128,1024]{1,0:T(8,128)(2,1)S(1)}, bf16[128,1024]{1,0:T(8,128)(2,1)S(1)}, u32[]{:S(2)}, u32[]{:S(2)}) %collective-permute-start.28) | collective-permute-done | bytes 262176 | tf_op jit(solution)/shard_map/ppermute | solution.py:17
  244.8 2.9 collective-permute-start.22
  247.7 2.7 collective-permute-done.26
  252.3 3.7 %collective-permute-done.25 = bf16[128,1024]{1,0:T(8,128)(2,1)S(1)} collective-permute-done((bf16[128,1024]{1,0:T(8,128)(2,1)S(1)}, bf16[128,1024]{1,0:T(8,128)(2,1)S(1)}, u32[]{:S(2)}, u32[]{:S(2)}) %collective-permute-start.25) | collective-permute-done | bytes 262176 | tf_op jit(solution)/shard_map/ppermute | solution.py:17
  258.0 6.0 %collective-permute-done.31 = bf16[128,1024]{1,0:T(8,128)(2,1)S(1)} collective-permute-done((bf16[128,1024]{1,0:T(8,128)(2,1)S(1)}, bf16[128,1024]{1,0:T(8,128)(2,1)S(1)}, u32[]{:S(2)}, u32[]{:S(2)}) %collective-permute-start.31) | collective-permute-done | bytes 262176 | tf_op jit(solution)/shard_map/ppermute | solution.py:17
  267.3 2.5 collective-permute-start.18
  269.8 3.1 %collective-permute-done.22 = bf16[128,1024]{1,0:T(8,128)(2,1)S(1)} collective-permute-done((bf16[128,1024]{1,0:T(8,128)(2,1)S(1)}, bf16[128,1024]{1,0:T(8,128)(2,1)S(1)}, u32[]{:S(2)}, u32[]{:S(2)}) %collective-permute-start.22) | collective-permute-done | bytes 262176 | tf_op jit(solution)/shard_map/ppermute | solution.py:17
  274.8 3.7 %collective-permute-done.21 = bf16[128,1024]{1,0:T(8,128)(2,1)S(1)} collective-permute-done((bf16[128,1024]{1,0:T(8,128)(2,1)S(1)}, bf16[128,1024]{1,0:T(8,128)(2,1)S(1)}, u32[]{:S(2)}, u32[]{:S(2)}) %collective-permute-start.21) | collective-permute-done | bytes 262176 | tf_op jit(solution)/shard_map/ppermute | solution.py:17
  281.6 2.6 collective-permute-done.20
  284.2 5.6 %collective-permute-done.19 = bf16[128,1024]{1,0:T(8,128)(2,1)S(1)} collective-permute-done((bf16[128,1024]{1,0:T(8,128)(2,1)S(1)}, bf16[128,1024]{1,0:T(8,128)(2,1)S(1)}, u32[]{:S(2)}, u32[]{:S(2)}) %collective-permute-start.19) | collective-permute-done | bytes 262176 | tf_op jit(solution)/shard_map/ppermute | solution.py:17
  289.8 5.6 %collective-permute-done.18 = bf16[128,1024]{1,0:T(8,128)(2,1)S(1)} collective-permute-done((bf16[128,1024]{1,0:T(8,128)(2,1)S(1)}, bf16[128,1024]{1,0:T(8,128)(2,1)S(1)}, u32[]{:S(2)}, u32[]{:S(2)}) %collective-permute-start.18) | collective-permute-done | bytes 262176 | tf_op jit(solution)/shard_map/ppermute | solution.py:17
  295.4 5.6 %collective-permute-done.17 = bf16[128,1024]{1,0:T(8,128)(2,1)S(1)} collective-permute-done((bf16[128,1024]{1,0:T(8,128)(2,1)S(1)}, bf16[128,1024]{1,0:T(8,128)(2,1)S(1)}, u32[]{:S(2)}, u32[]{:S(2)}) %collective-permute-start.17) | collective-permute-done | bytes 262176 | tf_op jit(solution)/shard_map/ppermute | solution.py:17
  301.0 6.0 %collective-permute-done.23 = bf16[128,1024]{1,0:T(8,128)(2,1)S(1)} collective-permute-done((bf16[128,1024]{1,0:T(8,128)(2,1)S(1)}, bf16[128,1024]{1,0:T(8,128)(2,1)S(1)}, u32[]{:S(2)}, u32[]{:S(2)}) %collective-permute-start.23) | collective-permute-done | bytes 262176 | tf_op jit(solution)/shard_map/ppermute | solution.py:17
  (167 shorter events, 123.1 us)
Async XLA Ops:
  0.6 46.6 %copy-start.2 = (bf16[128,1024]{1,0:T(8,128)(2,1)S(1)}, bf16[128,1024]{1,0:T(8,128)(2,1)}, u32[]{:S(2)}) copy-start(bf16[128,1024]{1,0:T(8,128)(2,1)} %param.7) | copy-start | bytes 786436
  1.8 88.6 %collective-permute-start.7 = (bf16[128,1024]{0,1:T(8,128)(2,1)S(1)}, bf16[128,1024]{0,1:T(8,128)(2,1)S(1)}, u32[]{:S(2)}, u32[]{:S(2)}) collective-permute-start(bf16[128,1024]{0,1:T(8,128)(2,1)S(1)} %copy.34), channel_id=1, source_target_pairs={{0,1},{1,2},{2,3},{3,4},{4,5},{5,6},{6,7},{7,8},{8,9},{9,10},{10,1... | collective-permute-start | bytes 786440 | tf_op jit(solution)/shard_map/ppermute | solution.py:17
  3.7 86.6 %collective-permute-start.6 = (bf16[128,1024]{0,1:T(8,128)(2,1)S(1)}, bf16[128,1024]{0,1:T(8,128)(2,1)S(1)}, u32[]{:S(2)}, u32[]{:S(2)}) collective-permute-start(bf16[128,1024]{0,1:T(8,128)(2,1)S(1)} %copy.34), channel_id=1, source_target_pairs={{0,2},{1,3},{2,4},{3,5},{4,6},{5,7},{6,8},{7,9},{8,10},{9,11},{10,... | collective-permute-start | bytes 786440 | tf_op jit(solution)/shard_map/ppermute | solution.py:17
  7.1 28.5 %collective-permute-start.10 = (bf16[128,1024]{1,0:T(8,128)(2,1)}, bf16[128,1024]{1,0:T(8,128)(2,1)S(1)}, u32[]{:S(2)}, u32[]{:S(2)}) collective-permute-start(bf16[128,1024]{1,0:T(8,128)(2,1)} %param.7), channel_id=1, source_target_pairs={{0,6},{1,7},{2,8},{3,9},{4,10},{5,11},{6,12},{7,13},{8,14},{9,15},... | collective-permute-start | bytes 786440 | tf_op jit(solution)/shard_map/ppermute | solution.py:17
  11.5 22.0 %collective-permute-start.9 = (bf16[128,1024]{1,0:T(8,128)(2,1)}, bf16[128,1024]{1,0:T(8,128)(2,1)S(1)}, u32[]{:S(2)}, u32[]{:S(2)}) collective-permute-start(bf16[128,1024]{1,0:T(8,128)(2,1)} %param.7), channel_id=1, source_target_pairs={{0,7},{1,8},{2,9},{3,10},{4,11},{5,12},{6,13},{7,14},{8,15},{9,16}... | collective-permute-start | bytes 786440 | tf_op jit(solution)/shard_map/ppermute | solution.py:17
  14.4 10.6 %collective-permute-start.8 = (bf16[128,1024]{1,0:T(8,128)(2,1)}, bf16[128,1024]{1,0:T(8,128)(2,1)S(1)}, u32[]{:S(2)}, u32[]{:S(2)}) collective-permute-start(bf16[128,1024]{1,0:T(8,128)(2,1)} %param.7), channel_id=1, source_target_pairs={{0,8},{1,9},{2,10},{3,11},{4,12},{5,13},{6,14},{7,15},{8,16},{9,17... | collective-permute-start | bytes 786440 | tf_op jit(solution)/shard_map/ppermute | solution.py:17
  25.0 15.1 %collective-permute-start.11 = (bf16[128,1024]{1,0:T(8,128)(2,1)}, bf16[128,1024]{1,0:T(8,128)(2,1)S(1)}, u32[]{:S(2)}, u32[]{:S(2)}) collective-permute-start(bf16[128,1024]{1,0:T(8,128)(2,1)} %param.7), channel_id=1, source_target_pairs={{0,5},{1,6},{2,7},{3,8},{4,9},{5,10},{6,11},{7,12},{8,13},{9,14},{... | collective-permute-start | bytes 786440 | tf_op jit(solution)/shard_map/ppermute | solution.py:17
  33.5 13.8 %collective-permute-start.12 = (bf16[128,1024]{1,0:T(8,128)(2,1)}, bf16[128,1024]{1,0:T(8,128)(2,1)S(1)}, u32[]{:S(2)}, u32[]{:S(2)}) collective-permute-start(bf16[128,1024]{1,0:T(8,128)(2,1)} %param.7), channel_id=1, source_target_pairs={{0,4},{1,5},{2,6},{3,7},{4,8},{5,9},{6,10},{7,11},{8,12},{9,13},{1... | collective-permute-start | bytes 786440 | tf_op jit(solution)/shard_map/ppermute | solution.py:17
  35.7 13.9 %collective-permute-start.13 = (bf16[128,1024]{1,0:T(8,128)(2,1)}, bf16[128,1024]{1,0:T(8,128)(2,1)S(1)}, u32[]{:S(2)}, u32[]{:S(2)}) collective-permute-start(bf16[128,1024]{1,0:T(8,128)(2,1)} %param.7), channel_id=1, source_target_pairs={{0,3},{1,4},{2,5},{3,6},{4,7},{5,8},{6,9},{7,10},{8,11},{9,12},{10... | collective-permute-start | bytes 786440 | tf_op jit(solution)/shard_map/ppermute | solution.py:17
  40.1 19.9 %collective-permute-start.14 = (bf16[128,1024]{1,0:T(8,128)(2,1)}, bf16[128,1024]{1,0:T(8,128)(2,1)S(1)}, u32[]{:S(2)}, u32[]{:S(2)}) collective-permute-start(bf16[128,1024]{1,0:T(8,128)(2,1)} %param.7), channel_id=1, source_target_pairs={{0,2},{1,3},{2,4},{3,5},{4,6},{5,7},{6,8},{7,9},{8,10},{9,11},{10,... | collective-permute-start | bytes 786440 | tf_op jit(solution)/shard_map/ppermute | solution.py:17
  47.2 16.3 %collective-permute-start.15 = (bf16[128,1024]{1,0:T(8,128)(2,1)S(1)}, bf16[128,1024]{1,0:T(8,128)(2,1)S(1)}, u32[]{:S(2)}, u32[]{:S(2)}) collective-permute-start(bf16[128,1024]{1,0:T(8,128)(2,1)S(1)} %copy-done.2), channel_id=1, source_target_pairs={{0,1},{1,2},{2,3},{3,4},{4,5},{5,6},{6,7},{7,8},{8,9},{9,10},{10,1... | collective-permute-start | bytes 786440 | tf_op jit(solution)/shard_map/ppermute | solution.py:17
  49.6 29.1 %collective-permute-start.2 = (bf16[128,1024]{0,1:T(8,128)(2,1)S(1)}, bf16[128,1024]{0,1:T(8,128)(2,1)S(1)}, u32[]{:S(2)}, u32[]{:S(2)}) collective-permute-start(bf16[128,1024]{0,1:T(8,128)(2,1)S(1)} %copy.34), channel_id=1, source_target_pairs={{0,6},{1,7},{2,8},{3,9},{4,10},{5,11},{6,12},{7,13},{8,14},{9,15},... | collective-permute-start | bytes 786440 | tf_op jit(solution)/shard_map/ppermute | solution.py:17
  60.0 10.9 %collective-permute-start = (bf16[128,1024]{0,1:T(8,128)(2,1)S(1)}, bf16[128,1024]{0,1:T(8,128)(2,1)S(1)}, u32[]{:S(2)}, u32[]{:S(2)}) collective-permute-start(bf16[128,1024]{0,1:T(8,128)(2,1)S(1)} %copy.34), channel_id=1, source_target_pairs={{0,8},{1,9},{2,10},{3,11},{4,12},{5,13},{6,14},{7,15},{8,16},{9,17... | collective-permute-start | bytes 786440 | tf_op jit(solution)/shard_map/ppermute | solution.py:17
  63.5 9.3 %collective-permute-start.1 = (bf16[128,1024]{0,1:T(8,128)(2,1)S(1)}, bf16[128,1024]{0,1:T(8,128)(2,1)S(1)}, u32[]{:S(2)}, u32[]{:S(2)}) collective-permute-start(bf16[128,1024]{0,1:T(8,128)(2,1)S(1)} %copy.34), channel_id=1, source_target_pairs={{0,7},{1,8},{2,9},{3,10},{4,11},{5,12},{6,13},{7,14},{8,15},{9,16}... | collective-permute-start | bytes 786440 | tf_op jit(solution)/shard_map/ppermute | solution.py:17
  66.3 24.2 %copy-start.1 = (bf16[1152,1024]{1,0:T(8,128)(2,1)}, bf16[1152,1024]{1,0:T(8,128)(2,1)S(1)}, u32[]{:S(2)}) copy-start(bf16[1152,1024]{1,0:T(8,128)(2,1)S(1)} %constant_dynamic-update-slice_fusion.11) | copy-start | bytes 7077892
  70.9 12.0 %collective-permute-start.3 = (bf16[128,1024]{0,1:T(8,128)(2,1)S(1)}, bf16[128,1024]{0,1:T(8,128)(2,1)S(1)}, u32[]{:S(2)}, u32[]{:S(2)}) collective-permute-start(bf16[128,1024]{0,1:T(8,128)(2,1)S(1)} %copy.34), channel_id=1, source_target_pairs={{0,5},{1,6},{2,7},{3,8},{4,9},{5,10},{6,11},{7,12},{8,13},{9,14},{... | collective-permute-start | bytes 786440 | tf_op jit(solution)/shard_map/ppermute | solution.py:17
  72.9 12.0 %collective-permute-start.4 = (bf16[128,1024]{0,1:T(8,128)(2,1)S(1)}, bf16[128,1024]{0,1:T(8,128)(2,1)S(1)}, u32[]{:S(2)}, u32[]{:S(2)}) collective-permute-start(bf16[128,1024]{0,1:T(8,128)(2,1)S(1)} %copy.34), channel_id=1, source_target_pairs={{0,4},{1,5},{2,6},{3,7},{4,8},{5,9},{6,10},{7,11},{8,12},{9,13},{1... | collective-permute-start | bytes 786440 | tf_op jit(solution)/shard_map/ppermute | solution.py:17
  78.7 11.6 %collective-permute-start.5 = (bf16[128,1024]{0,1:T(8,128)(2,1)S(1)}, bf16[128,1024]{0,1:T(8,128)(2,1)S(1)}, u32[]{:S(2)}, u32[]{:S(2)}) collective-permute-start(bf16[128,1024]{0,1:T(8,128)(2,1)S(1)} %copy.34), channel_id=1, source_target_pairs={{0,3},{1,4},{2,5},{3,6},{4,7},{5,8},{6,9},{7,10},{8,11},{9,12},{10... | collective-permute-start | bytes 786440 | tf_op jit(solution)/shard_map/ppermute | solution.py:17
  90.6 1.6 copy-start.3
  210.5 18.8 %copy-start = (bf16[1152,1024]{1,0:T(8,128)(2,1)S(1)}, bf16[1152,1024]{1,0:T(8,128)(2,1)}, u32[]{:S(2)}) copy-start(bf16[1152,1024]{1,0:T(8,128)(2,1)} %get-tuple-element.178) | copy-start | bytes 7077892
  210.8 16.6 %collective-permute-start.24 = (bf16[128,1024]{1,0:T(8,128)(2,1)S(1)}, bf16[128,1024]{1,0:T(8,128)(2,1)S(1)}, u32[]{:S(2)}, u32[]{:S(2)}) collective-permute-start(bf16[128,1024]{1,0:T(8,128)(2,1)S(1)} %get-tuple-element.279), channel_id=1, source_target_pairs={{1,0},{2,1},{3,2},{4,3},{5,4},{6,5},{7,6},{8,7},{9,8},{10,9},{11,1... | collective-permute-start | bytes 786440 | tf_op jit(solution)/shard_map/ppermute | solution.py:17
  217.8 11.7 %collective-permute-start.30 = (bf16[128,1024]{1,0:T(8,128)(2,1)S(1)}, bf16[128,1024]{1,0:T(8,128)(2,1)S(1)}, u32[]{:S(2)}, u32[]{:S(2)}) collective-permute-start(bf16[128,1024]{1,0:T(8,128)(2,1)S(1)} %get-tuple-element.280), channel_id=1, source_target_pairs={{7,0},{8,1},{9,2},{10,3},{11,4},{12,5},{13,6},{14,7},{15,8},{16,9}... | collective-permute-start | bytes 786440 | tf_op jit(solution)/shard_map/ppermute | solution.py:17
  220.1 12.8 %collective-permute-start.29 = (bf16[128,1024]{1,0:T(8,128)(2,1)S(1)}, bf16[128,1024]{1,0:T(8,128)(2,1)S(1)}, u32[]{:S(2)}, u32[]{:S(2)}) collective-permute-start(bf16[128,1024]{1,0:T(8,128)(2,1)S(1)} %get-tuple-element.281), channel_id=1, source_target_pairs={{6,0},{7,1},{8,2},{9,3},{10,4},{11,5},{12,6},{13,7},{14,8},{15,9},... | collective-permute-start | bytes 786440 | tf_op jit(solution)/shard_map/ppermute | solution.py:17
  223.5 17.7 %collective-permute-start.28 = (bf16[128,1024]{1,0:T(8,128)(2,1)S(1)}, bf16[128,1024]{1,0:T(8,128)(2,1)S(1)}, u32[]{:S(2)}, u32[]{:S(2)}) collective-permute-start(bf16[128,1024]{1,0:T(8,128)(2,1)S(1)} %get-tuple-element.282), channel_id=1, source_target_pairs={{5,0},{6,1},{7,2},{8,3},{9,4},{10,5},{11,6},{12,7},{13,8},{14,9},{... | collective-permute-start | bytes 786440 | tf_op jit(solution)/shard_map/ppermute | solution.py:17
  225.4 19.4 %collective-permute-start.27 = (bf16[128,1024]{1,0:T(8,128)(2,1)S(1)}, bf16[128,1024]{1,0:T(8,128)(2,1)S(1)}, u32[]{:S(2)}, u32[]{:S(2)}) collective-permute-start(bf16[128,1024]{1,0:T(8,128)(2,1)S(1)} %get-tuple-element.283), channel_id=1, source_target_pairs={{4,0},{5,1},{6,2},{7,3},{8,4},{9,5},{10,6},{11,7},{12,8},{13,9},{1... | collective-permute-start | bytes 786440 | tf_op jit(solution)/shard_map/ppermute | solution.py:17
  227.4 23.0 %collective-permute-start.26 = (bf16[128,1024]{1,0:T(8,128)(2,1)S(1)}, bf16[128,1024]{1,0:T(8,128)(2,1)S(1)}, u32[]{:S(2)}, u32[]{:S(2)}) collective-permute-start(bf16[128,1024]{1,0:T(8,128)(2,1)S(1)} %get-tuple-element.284), channel_id=1, source_target_pairs={{3,0},{4,1},{5,2},{6,3},{7,4},{8,5},{9,6},{10,7},{11,8},{12,9},{13... | collective-permute-start | bytes 786440 | tf_op jit(solution)/shard_map/ppermute | solution.py:17
  229.5 26.6 %collective-permute-start.25 = (bf16[128,1024]{1,0:T(8,128)(2,1)S(1)}, bf16[128,1024]{1,0:T(8,128)(2,1)S(1)}, u32[]{:S(2)}, u32[]{:S(2)}) collective-permute-start(bf16[128,1024]{1,0:T(8,128)(2,1)S(1)} %get-tuple-element.285), channel_id=1, source_target_pairs={{2,0},{3,1},{4,2},{5,3},{6,4},{7,5},{8,6},{9,7},{10,8},{11,9},{12,... | collective-permute-start | bytes 786440 | tf_op jit(solution)/shard_map/ppermute | solution.py:17
  232.9 31.0 %collective-permute-start.31 = (bf16[128,1024]{1,0:T(8,128)(2,1)S(1)}, bf16[128,1024]{1,0:T(8,128)(2,1)S(1)}, u32[]{:S(2)}, u32[]{:S(2)}) collective-permute-start(bf16[128,1024]{1,0:T(8,128)(2,1)S(1)} %get-tuple-element.286), channel_id=1, source_target_pairs={{8,0},{9,1},{10,2},{11,3},{12,4},{13,5},{14,6},{15,7},{16,8},{17,9... | collective-permute-start | bytes 786440 | tf_op jit(solution)/shard_map/ppermute | solution.py:17
  241.2 26.1 %collective-permute-start.16 = (bf16[128,1024]{1,0:T(8,128)(2,1)S(1)}, bf16[128,1024]{1,0:T(8,128)(2,1)S(1)}, u32[]{:S(2)}, u32[]{:S(2)}) collective-permute-start(bf16[128,1024]{1,0:T(8,128)(2,1)S(1)} %get-tuple-element.287), channel_id=1, source_target_pairs={{1,0},{2,1},{3,2},{4,3},{5,4},{6,5},{7,6},{8,7},{9,8},{10,9},{11,1... | collective-permute-start | bytes 786440 | tf_op jit(solution)/shard_map/ppermute | solution.py:17
  244.8 28.1 %collective-permute-start.22 = (bf16[128,1024]{1,0:T(8,128)(2,1)S(1)}, bf16[128,1024]{1,0:T(8,128)(2,1)S(1)}, u32[]{:S(2)}, u32[]{:S(2)}) collective-permute-start(bf16[128,1024]{1,0:T(8,128)(2,1)S(1)} %get-tuple-element.288), channel_id=1, source_target_pairs={{7,0},{8,1},{9,2},{10,3},{11,4},{12,5},{13,6},{14,7},{15,8},{16,9}... | collective-permute-start | bytes 786440 | tf_op jit(solution)/shard_map/ppermute | solution.py:17
  250.4 28.1 %collective-permute-start.21 = (bf16[128,1024]{1,0:T(8,128)(2,1)S(1)}, bf16[128,1024]{1,0:T(8,128)(2,1)S(1)}, u32[]{:S(2)}, u32[]{:S(2)}) collective-permute-start(bf16[128,1024]{1,0:T(8,128)(2,1)S(1)} %get-tuple-element.289), channel_id=1, source_target_pairs={{6,0},{7,1},{8,2},{9,3},{10,4},{11,5},{12,6},{13,7},{14,8},{15,9},... | collective-permute-start | bytes 786440 | tf_op jit(solution)/shard_map/ppermute | solution.py:17
  256.1 28.1 %collective-permute-start.20 = (bf16[128,1024]{1,0:T(8,128)(2,1)S(1)}, bf16[128,1024]{1,0:T(8,128)(2,1)S(1)}, u32[]{:S(2)}, u32[]{:S(2)}) collective-permute-start(bf16[128,1024]{1,0:T(8,128)(2,1)S(1)} %get-tuple-element.290), channel_id=1, source_target_pairs={{5,0},{6,1},{7,2},{8,3},{9,4},{10,5},{11,6},{12,7},{13,8},{14,9},{... | collective-permute-start | bytes 786440 | tf_op jit(solution)/shard_map/ppermute | solution.py:17
  263.9 25.8 %collective-permute-start.19 = (bf16[128,1024]{1,0:T(8,128)(2,1)S(1)}, bf16[128,1024]{1,0:T(8,128)(2,1)S(1)}, u32[]{:S(2)}, u32[]{:S(2)}) collective-permute-start(bf16[128,1024]{1,0:T(8,128)(2,1)S(1)} %get-tuple-element.291), channel_id=1, source_target_pairs={{4,0},{5,1},{6,2},{7,3},{8,4},{9,5},{10,6},{11,7},{12,8},{13,9},{1... | collective-permute-start | bytes 786440 | tf_op jit(solution)/shard_map/ppermute | solution.py:17
  267.3 28.1 %collective-permute-start.18 = (bf16[128,1024]{1,0:T(8,128)(2,1)S(1)}, bf16[128,1024]{1,0:T(8,128)(2,1)S(1)}, u32[]{:S(2)}, u32[]{:S(2)}) collective-permute-start(bf16[128,1024]{1,0:T(8,128)(2,1)S(1)} %get-tuple-element.292), channel_id=1, source_target_pairs={{3,0},{4,1},{5,2},{6,3},{7,4},{8,5},{9,6},{10,7},{11,8},{12,9},{13... | collective-permute-start | bytes 786440 | tf_op jit(solution)/shard_map/ppermute | solution.py:17
  272.9 28.1 %collective-permute-start.17 = (bf16[128,1024]{1,0:T(8,128)(2,1)S(1)}, bf16[128,1024]{1,0:T(8,128)(2,1)S(1)}, u32[]{:S(2)}, u32[]{:S(2)}) collective-permute-start(bf16[128,1024]{1,0:T(8,128)(2,1)S(1)} %get-tuple-element.293), channel_id=1, source_target_pairs={{2,0},{3,1},{4,2},{5,3},{6,4},{7,5},{8,6},{9,7},{10,8},{11,9},{12,... | collective-permute-start | bytes 786440 | tf_op jit(solution)/shard_map/ppermute | solution.py:17
  278.5 28.5 %collective-permute-start.23 = (bf16[128,1024]{1,0:T(8,128)(2,1)S(1)}, bf16[128,1024]{1,0:T(8,128)(2,1)S(1)}, u32[]{:S(2)}, u32[]{:S(2)}) collective-permute-start(bf16[128,1024]{1,0:T(8,128)(2,1)S(1)} %get-tuple-element.294), channel_id=1, source_target_pairs={{8,0},{9,1},{10,2},{11,3},{12,4},{13,5},{14,6},{15,7},{16,8},{17,9... | collective-permute-start | bytes 786440 | tf_op jit(solution)/shard_map/ppermute | solution.py:17
where the time goes:
time: 311 us; the launch traced here: 308 us
  starting transfers between devices  104 us (33%)
  matrix products  85.4 us (27%)
  waiting for transfers between devices  78.5 us (25%)
  local copies, waits for them, and re-layouts  29.2 us (9%)
  other arithmetic  9.17 us (3%)
    ppermute x32, starting transfers between devices, from_behind(): return lax.ppermute(value, axis, pairs)  104 us
    ppermute x32, waiting for transfers between devices, from_behind(): return lax.ppermute(value, axis, pairs)  78.5 us
    sub x8, matrix products, group_step(): expo = jnp.exp(scores - peak)  20.6 us
    dot_general x8, matrix products, group_step(): jnp.einsum('rij,ird->jd', probs_low, grad_group, preferred_element_type=j...  16.5 us
    dot_general x8, matrix products, group_step(): jnp.einsum('rij,jd->ird', probs_low, value_group, preferred_element_type=...  15.6 us
    dot_general x8, matrix products, group_step(): jnp.einsum('ird,jd->rij', grad_group, value_group, preferred_element_type...  14.1 us
    dot_general x8, matrix products, group_step(): jnp.einsum('rij,jd->ird', grad_scores, key_group, preferred_element_type=...  10 us
    dot_general x8, matrix products, group_step(): jnp.einsum('rij,ird->jd', grad_scores, query_group, preferred_element_typ...  8.59 us
  transfers between devices with their start and end apart: 32, of which 19 were waited for; matrix products, arithmetic and copies ran while one was open for 1% of the time, Pallas kernels for 0%

commit v1 on v0

v1 whole, which is shorter than its diff:
```python
import functools

import jax
import jax.numpy as jnp
from jax import lax
from jax.experimental import pallas as pl
from jax.experimental.pallas import tpu as pltpu
from jax.sharding import PartitionSpec as P

HEAD_DIM = 128
WINDOW = 1024
QUERY_SCALE = 168
LOG2E = 1.4426950408889634

masked_score = -1e30
MESH = pl.DeviceIdType.MESH


def contract(left, right, dims):
    return lax.dot_general(left, right, (dims, ((), ())), preferred_element_type=jnp.float32)


def kernel(
    team, repeat, tensor_size, total,
    q_hbm, k_hbm, v_hbm, g_hbm,
    att_hbm, gq_hbm, gk_hbm, gv_hbm,
    qb, gb, kv, kvt, dk, dv, att, gq, back, later, fin, land, work, pbuf, dbuf,
    in_send, in_recv, fwd_send, fwd_recv, out_send, out_recv,
    back_send, back_recv, fin_send, fin_recv, store_sem,
):
    rows = q_hbm.shape[0]
    width = repeat * HEAD_DIM
    scale = QUERY_SCALE ** (-0.5)
    me = lax.axis_index("dp") * tensor_size + lax.axis_index("tensor")
    member = lax.rem(me, team)
    base = me - member
    has_prev = me >= team
    has_next = me + team < total

    def place(index):
        return (lax.div(index, tensor_size), lax.rem(index, tensor_size))

    def peer(step):
        return lax.rem(member + step, team)

    barrier = pltpu.get_barrier_semaphore()
    for step in range(1, team):
        pl.semaphore_signal(barrier, inc=1, device_id=place(base + peer(step)), device_id_type=MESH)

    @pl.when(has_prev)
    def _():
        pl.semaphore_signal(barrier, inc=1, device_id=place(me - team), device_id_type=MESH)

    @pl.when(has_next)
    def _():
        pl.semaphore_signal(barrier, inc=1, device_id=place(me + team), device_id_type=MESH)

    pl.semaphore_wait(barrier, team - 1 + has_prev.astype(jnp.int32) + has_next.astype(jnp.int32))

    def wide(index):
        return pl.ds(pl.multiple_of(index * width, width), width)

    def narrow(index):
        return pl.ds(pl.multiple_of(index * HEAD_DIM, HEAD_DIM), HEAD_DIM)

    k_half = pl.ds(0, HEAD_DIM)
    v_half = pl.ds(HEAD_DIM, HEAD_DIM)

    def pieces(to, slot):
        return (
            (k_hbm.at[:, narrow(to)], kv.at[team + slot, :, k_half]),
            (v_hbm.at[:, narrow(to)], kv.at[team + slot, :, v_half]),
            (q_hbm.at[:, wide(to)], qb.at[slot]),
            (g_hbm.at[:, wide(to)], gb.at[slot]),
        )

    def in_copy(kind, to):
        src, dst = pieces(to, member)[kind]
        return pltpu.make_async_remote_copy(
            src_ref=src, dst_ref=dst,
            send_sem=in_send.at[kind, to], recv_sem=in_recv.at[kind, member],
            device_id=place(base + to), device_id_type=MESH,
        )

    def in_wait(kind, source):
        src, dst = pieces(member, source)[kind]
        pltpu.make_async_copy(src, dst, in_recv.at[kind, source]).wait()

    for kind in range(4):
        src, dst = pieces(member, member)[kind]
        pltpu.make_async_copy(src, dst, in_recv.at[kind, member]).start()
    for kinds in ((0, 1), (2, 3)):
        for step in range(1, team):
            for kind in kinds:
                in_copy(kind, peer(step)).start()

    dk[...] = jnp.zeros_like(dk)
    dv[...] = jnp.zeros_like(dv)

    def fwd_copy(slot):
        return pltpu.make_async_remote_copy(
            src_ref=kv.at[team + slot], dst_ref=kv.at[slot],
            send_sem=fwd_send.at[slot], recv_sem=fwd_recv.at[slot],
            device_id=place(me + team), device_id_type=MESH,
        )

    for step in range(team):
        source = peer(step)
        in_wait(0, source)
        in_wait(1, source)

        @pl.when(has_next)
        def _():
            fwd_copy(source).start()

    def turn(slot):
        kvt[:, pl.ds(pl.multiple_of(slot * rows, rows), rows)] = kv[slot].T

    @pl.loop(0, team)
    def _(slot):
        turn(team + slot)

    @pl.when(jnp.logical_not(has_prev))
    def _():
        kv[pl.ds(0, team)] = jnp.zeros((team,) + kv.shape[1:], kv.dtype)

    @pl.loop(0, team)
    def _(step):
        slot = peer(step)

        @pl.when(has_prev)
        def _():
            pltpu.make_async_copy(kv.at[team + slot], kv.at[slot], fwd_recv.at[slot]).wait()

        turn(slot)

    span = (team + 1) * rows
    key_at = lax.broadcasted_iota(jnp.int32, (rows, repeat * rows), 0)
    query_at = lax.rem(lax.broadcasted_iota(jnp.int32, (rows, repeat * rows), 1), rows)
    factor = scale * LOG2E

    def stack(block):
        return jnp.concatenate(
            [block[:, h * HEAD_DIM : (h + 1) * HEAD_DIM] for h in range(repeat)], axis=0
        )

    def unstack(block):
        return jnp.concatenate([block[h * rows : (h + 1) * rows] for h in range(repeat)], axis=1)

    def out_copy(kind, to):
        buf, ref = ((att, att_hbm), (gq, gq_hbm))[kind]
        return pltpu.make_async_remote_copy(
            src_ref=buf.at[to], dst_ref=ref.at[:, wide(member)],
            send_sem=out_send.at[kind, to], recv_sem=out_recv.at[kind, member],
            device_id=place(base + to), device_id_type=MESH,
        )

    def out_own(kind):
        buf, ref = ((att, att_hbm), (gq, gq_hbm))[kind]
        return pltpu.make_async_copy(
            buf.at[member], ref.at[:, wide(member)], out_recv.at[kind, member]
        )

    def ship(kind, to):
        @pl.when(to != member)
        def _():
            out_copy(kind, to).start()

        @pl.when(to == member)
        def _():
            out_own(kind).start()

    @pl.loop(0, team)
    def _(step):
        b = peer(step)
        in_wait(2, b)
        in_wait(3, b)
        q2 = stack(qb[b])
        g2 = stack(gb[b])
        q2t = q2.T
        g2t = g2.T
        cols = pl.ds(pl.multiple_of(b * rows, rows), span)
        gone = [jnp.logical_and(jnp.logical_not(has_prev), b + r < team) for r in range(team)]
        gone.append(None)
        peak = None
        for r in range(team + 1):
            part = contract(kv[b + r, :, :HEAD_DIM], q2t, ((1,), (0,)))
            if r == 0:
                part = jnp.where(key_at > query_at, part, masked_score)
            if r == team:
                part = jnp.where(key_at <= query_at, part, masked_score)
            work[r] = part
            top = jnp.max(part.reshape(rows // 8, 8, width), axis=0)
            if r < team:
                top = jnp.where(gone[r], masked_score, top)
            peak = top if peak is None else jnp.maximum(peak, top)
        low = jnp.max(peak, axis=0, keepdims=True) * factor
        denom = None
        for r in range(team + 1):
            shift = low if r == team else jnp.where(gone[r], -masked_score, low)
            expo = jnp.exp2(work[r] * factor - shift)
            work[r] = expo
            part = jnp.sum(expo.reshape(rows // 8, 8, width), axis=0)
            denom = part if denom is None else denom + part
        inverse = 1.0 / jnp.sum(denom, axis=0, keepdims=True)
        for r in range(team + 1):
            probs = work[r] * inverse
            work[r] = probs
            pbuf[r * rows : (r + 1) * rows] = probs.astype(jnp.bfloat16)
        out_t = contract(kvt[HEAD_DIM:, cols], pbuf[...], ((1,), (0,)))
        att[b] = unstack(out_t.T).astype(jnp.bfloat16)
        ship(0, b)
        delta = jnp.sum(g2t.astype(jnp.float32) * out_t, axis=0, keepdims=True)
        for r in range(team + 1):
            grad_probs = contract(kv[b + r, :, HEAD_DIM:], g2t, ((1,), (0,)))
            dbuf[r * rows : (r + 1) * rows] = (work[r] * (grad_probs - delta)).astype(jnp.bfloat16)
        dq_t = contract(kvt[:HEAD_DIM, cols], dbuf[...], ((1,), (0,))) * scale
        gq[b] = unstack(dq_t.T).astype(jnp.bfloat16)
        ship(1, b)
        dk[cols, :] += contract(dbuf[...], q2, ((1,), (0,)))
        dv[cols, :] += contract(pbuf[...], g2, ((1,), (0,)))

    def back_copy(slot):
        return pltpu.make_async_remote_copy(
            src_ref=back.at[slot], dst_ref=later.at[slot],
            send_sem=back_send.at[slot], recv_sem=back_recv.at[slot],
            device_id=place(me - team), device_id_type=MESH,
        )

    def sums(slot):
        at = pl.ds(pl.multiple_of(slot * rows, rows), rows)
        return jnp.concatenate([dk[at, :] * scale, dv[at, :]], axis=1)

    @pl.when(has_prev)
    def _():
        @pl.loop(0, team)
        def _(step):
            slot = peer(step)
            back[slot] = sums(slot).astype(jnp.bfloat16)
            back_copy(slot).start()

    def fin_copy(to):
        return pltpu.make_async_remote_copy(
            src_ref=fin.at[to], dst_ref=land.at[member],
            send_sem=fin_send.at[to], recv_sem=fin_recv.at[member],
            device_id=place(base + to), device_id_type=MESH,
        )

    def fin_own():
        return pltpu.make_async_copy(fin.at[member], land.at[member], fin_recv.at[member])

    @pl.when(jnp.logical_not(has_next))
    def _():
        later[...] = jnp.zeros_like(later)

    @pl.loop(0, team)
    def _(step):
        slot = peer(step)

        @pl.when(has_next)
        def _():
            pltpu.make_async_copy(back.at[slot], later.at[slot], back_recv.at[slot]).wait()

        fin[slot] = (sums(team + slot) + later[slot].astype(jnp.float32)).astype(jnp.bfloat16)

        @pl.when(slot != member)
        def _():
            fin_copy(slot).start()

        @pl.when(slot == member)
        def _():
            fin_own().start()

    for step in range(team):
        source = lax.rem(member + team - step, team)
        pltpu.make_async_copy(fin.at[source], land.at[source], fin_recv.at[source]).wait()
        gk = pltpu.make_async_copy(
            land.at[source, :, k_half], gk_hbm.at[:, narrow(source)], store_sem.at[0, source]
        )
        gv = pltpu.make_async_copy(
            land.at[source, :, v_half], gv_hbm.at[:, narrow(source)], store_sem.at[1, source]
        )
        gk.start()
        gv.start()

    for step in range(team):
        source = peer(step)
        for kind in range(2):
            buf, ref = ((att, att_hbm), (gq, gq_hbm))[kind]
            pltpu.make_async_copy(
                buf.at[source], ref.at[:, wide(source)], out_recv.at[kind, source]
            ).wait()
        pltpu.make_async_copy(
            land.at[source, :, k_half], gk_hbm.at[:, narrow(source)], store_sem.at[0, source]
        ).wait()
        pltpu.make_async_copy(
            land.at[source, :, v_half], gv_hbm.at[:, narrow(source)], store_sem.at[1, source]
        ).wait()
    for step in range(1, team):
        to = peer(step)
        for kind in range(4):
            in_copy(kind, to).wait_send()
        for kind in range(2):
            out_copy(kind, to).wait_send()
        fin_copy(to).wait_send()

    @pl.when(has_next)
    def _():
        for slot in range(team):
            fwd_copy(slot).wait_send()

    @pl.when(has_prev)
    def _():
        for slot in range(team):
            back_copy(slot).wait_send()


def local(tensor_size, total, queries, key_rows, value_rows, out_grad):
    rows = queries.shape[0]
    team = WINDOW // rows
    repeat = queries.shape[1] // key_rows.shape[1]
    width = repeat * HEAD_DIM
    assert key_rows.shape[1] == team * HEAD_DIM
    bf16, f32 = jnp.bfloat16, jnp.float32
    dma = pltpu.SemaphoreType.DMA
    pairs = team * (team + 1) * rows * rows * repeat
    return pl.pallas_call(
        functools.partial(kernel, team, repeat, tensor_size, total),
        out_shape=tuple(
            jax.ShapeDtypeStruct(a.shape, bf16) for a in (queries, queries, key_rows, value_rows)
        ),
        in_specs=[pl.BlockSpec(memory_space=pl.ANY)] * 4,
        out_specs=(pl.BlockSpec(memory_space=pl.ANY),) * 4,
        scratch_shapes=[
            pltpu.VMEM((team, rows, width), bf16),
            pltpu.VMEM((team, rows, width), bf16),
            pltpu.VMEM((2 * team, rows, 2 * HEAD_DIM), bf16),
            pltpu.VMEM((2 * HEAD_DIM, 2 * team * rows), bf16),
            pltpu.VMEM((2 * team * rows, HEAD_DIM), f32),
            pltpu.VMEM((2 * team * rows, HEAD_DIM), f32),
            pltpu.VMEM((team, rows, width), bf16),
            pltpu.VMEM((team, rows, width), bf16),
            pltpu.VMEM((team, rows, 2 * HEAD_DIM), bf16),
            pltpu.VMEM((team, rows, 2 * HEAD_DIM), bf16),
            pltpu.VMEM((team, rows, 2 * HEAD_DIM), bf16),
            pltpu.VMEM((team, rows, 2 * HEAD_DIM), bf16),
            pltpu.VMEM((team + 1, rows, width), f32),
            pltpu.VMEM(((team + 1) * rows, width), bf16),
            pltpu.VMEM(((team + 1) * rows, width), bf16),
            dma((4, team)), dma((4, team)),
            dma((team,)), dma((team,)),
            dma((2, team)), dma((2, team)),
            dma((team,)), dma((team,)),
            dma((team,)), dma((team,)),
            dma((2, team)),
        ],
        compiler_params=pltpu.CompilerParams(
            collective_id=0, has_side_effects=True, vmem_limit_bytes=48 * 1024 * 1024
        ),
        cost_estimate=pl.CostEstimate(
            flops=12 * pairs * HEAD_DIM, bytes_accessed=12 * queries.size, transcendentals=pairs
        ),
    )(queries, key_rows, value_rows, out_grad)


def solution(mesh):
    spec = P(("dp", "tensor"), None)
    tensor_size = mesh.shape["tensor"]
    total = mesh.shape["dp"] * tensor_size
    return jax.shard_map(
        functools.partial(local, tensor_size, total),
        mesh=mesh, in_specs=(spec,) * 4, out_specs=(spec,) * 4, check_vma=False,
    )
```

time: 311 us -> 65 us (0.21)
  the two profiles are of different devices: /device:TPU:16 before, /device:TPU:1 now
where the time goes in v1:
time: 65 us; the launch traced here: 64.7 us
  Pallas kernels  57.1 us (88%)
  local copies, waits for them, and re-layouts  6.97 us (11%)
  between operations  0.65 us (1%)
    pallas_call x1, Pallas kernels, local(): pl.pallas_call(functools.partial(kernel, team, repeat, tensor_size, total...  57.1 us
    unnamed x12, local copies, waits for them, and re-layouts  6.97 us

profile of v1, /device:TPU:1, one launch (start us, length us, event | category | flops | bytes accessed | tf_op | source)
XLA Modules:
  0.0 64.7 jit_solution(13288540213190290863)
XLA Ops:
  0.6 0.0 copy-start
  0.6 1.0 %copy-done = bf16[128,2048]{1,0:T(8,128)(2,1)S(1)} copy-done((bf16[128,2048]{1,0:T(8,128)(2,1)S(1)}, bf16[128,2048]{1,0:T(8,128)(2,1)}, u32[]{:S(2)}) %copy-start) | copy-done | bytes 524312
  1.7 0.0 copy-start.1
  1.7 1.0 %copy-done.1 = bf16[128,2048]{1,0:T(8,128)(2,1)S(1)} copy-done((bf16[128,2048]{1,0:T(8,128)(2,1)S(1)}, bf16[128,2048]{1,0:T(8,128)(2,1)}, u32[]{:S(2)}) %copy-start.1) | copy-done | bytes 524312
  2.7 0.0 copy-start.2
  2.7 0.9 %copy-done.2 = bf16[128,1024]{1,0:T(8,128)(2,1)S(1)} copy-done((bf16[128,1024]{1,0:T(8,128)(2,1)S(1)}, bf16[128,1024]{1,0:T(8,128)(2,1)}, u32[]{:S(2)}) %copy-start.2) | copy-done | bytes 262168
  3.7 0.0 copy-start.3
  3.7 0.9 %copy-done.3 = bf16[128,1024]{1,0:T(8,128)(2,1)S(1)} copy-done((bf16[128,1024]{1,0:T(8,128)(2,1)S(1)}, bf16[128,1024]{1,0:T(8,128)(2,1)}, u32[]{:S(2)}) %copy-start.3) | copy-done | bytes 262168
  4.6 57.1 %shard_map.75 = (bf16[128,2048]{1,0:T(8,128)(2,1)S(1)}, bf16[128,2048]{1,0:T(8,128)(2,1)S(1)}, bf16[128,1024]{1,0:T(8,128)(2,1)S(1)}, bf16[128,1024]{1,0:T(8,128)(2,1)S(1)}) custom-call(bf16[128,2048]{1,0:T(8,128)(2,1)S(1)} %copy-done, bf16[128,1024]{1,0:T(8,128)(2,1)S(1)} %copy-done.2, bf16[128,1024]{1,0:T(8,128)(2,1)S(1)} %copy-done.3, ...), custom_call_target="tpu_custom_call" | custom-call | flops 3623878656 | bytes 3145728 | tf_op jit(solution)/shard_map/pallas_call | solution.py:327
  61.7 0.8 %copy.12 = bf16[128,2048]{1,0:T(8,128)(2,1)} copy(bf16[128,2048]{1,0:T(8,128)(2,1)S(1)} %get-tuple-element.8) | data formatting | bytes 1048576
  62.5 0.8 %copy.13 = bf16[128,2048]{1,0:T(8,128)(2,1)} copy(bf16[128,2048]{1,0:T(8,128)(2,1)S(1)} %get-tuple-element.9) | data formatting | bytes 1048576
  63.3 0.7 %copy.14 = bf16[128,1024]{1,0:T(8,128)(2,1)} copy(bf16[128,1024]{1,0:T(8,128)(2,1)S(1)} %get-tuple-element.10) | data formatting | bytes 524288
  64.0 0.7 %copy.15 = bf16[128,1024]{1,0:T(8,128)(2,1)} copy(bf16[128,1024]{1,0:T(8,128)(2,1)S(1)} %get-tuple-element.11) | data formatting | bytes 524288
Async XLA Ops:
  0.6 1.0 %copy-start = (bf16[128,2048]{1,0:T(8,128)(2,1)S(1)}, bf16[128,2048]{1,0:T(8,128)(2,1)}, u32[]{:S(2)}) copy-start(bf16[128,2048]{1,0:T(8,128)(2,1)} %q_hbm.1) | copy-start | bytes 1572868
  1.7 1.0 %copy-start.1 = (bf16[128,2048]{1,0:T(8,128)(2,1)S(1)}, bf16[128,2048]{1,0:T(8,128)(2,1)}, u32[]{:S(2)}) copy-start(bf16[128,2048]{1,0:T(8,128)(2,1)} %g_hbm.1) | copy-start | bytes 1572868
  2.7 0.9 %copy-start.2 = (bf16[128,1024]{1,0:T(8,128)(2,1)S(1)}, bf16[128,1024]{1,0:T(8,128)(2,1)}, u32[]{:S(2)}) copy-start(bf16[128,1024]{1,0:T(8,128)(2,1)} %k_hbm.1) | copy-start | bytes 786436
  3.7 0.9 %copy-start.3 = (bf16[128,1024]{1,0:T(8,128)(2,1)S(1)}, bf16[128,1024]{1,0:T(8,128)(2,1)}, u32[]{:S(2)}) copy-start(bf16[128,1024]{1,0:T(8,128)(2,1)} %v_hbm.1) | copy-start | bytes 786436

commit v2 on v1

--- a/solution.py
+++ b/solution.py
@@ -206,19 +206,17 @@
         for r in range(team + 1):
             probs = work[r] * inverse
             work[r] = probs
-            pbuf[r * rows : (r + 1) * rows] = probs.astype(jnp.bfloat16)
-        out_t = contract(kvt[HEAD_DIM:, cols], pbuf[...], ((1,), (0,)))
+            pbuf[b, r * rows : (r + 1) * rows] = probs.astype(jnp.bfloat16)
+        out_t = contract(kvt[HEAD_DIM:, cols], pbuf[b], ((1,), (0,)))
         att[b] = unstack(out_t.T).astype(jnp.bfloat16)
         ship(0, b)
         delta = jnp.sum(g2t.astype(jnp.float32) * out_t, axis=0, keepdims=True)
         for r in range(team + 1):
             grad_probs = contract(kv[b + r, :, HEAD_DIM:], g2t, ((1,), (0,)))
-            dbuf[r * rows : (r + 1) * rows] = (work[r] * (grad_probs - delta)).astype(jnp.bfloat16)
-        dq_t = contract(kvt[:HEAD_DIM, cols], dbuf[...], ((1,), (0,))) * scale
+            dbuf[b, r * rows : (r + 1) * rows] = (work[r] * (grad_probs - delta)).astype(jnp.bfloat16)
+        dq_t = contract(kvt[:HEAD_DIM, cols], dbuf[b], ((1,), (0,))) * scale
         gq[b] = unstack(dq_t.T).astype(jnp.bfloat16)
         ship(1, b)
-        dk[cols, :] += contract(dbuf[...], q2, ((1,), (0,)))
-        dv[cols, :] += contract(pbuf[...], g2, ((1,), (0,)))
 
     def back_copy(slot):
         return pltpu.make_async_remote_copy(
@@ -231,13 +229,16 @@
         at = pl.ds(pl.multiple_of(slot * rows, rows), rows)
         return jnp.concatenate([dk[at, :] * scale, dv[at, :]], axis=1)
 
-    @pl.when(has_prev)
-    def _():
-        @pl.loop(0, team)
-        def _(step):
-            slot = peer(step)
-            back[slot] = sums(slot).astype(jnp.bfloat16)
-            back_copy(slot).start()
+    @pl.loop(0, team)
+    def _(b):
+        at = pl.ds(pl.multiple_of(b * rows, rows), span)
+        dk[at, :] += contract(dbuf[b], stack(qb[b]), ((1,), (0,)))
+        dv[at, :] += contract(pbuf[b], stack(gb[b]), ((1,), (0,)))
+
+        @pl.when(has_prev)
+        def _():
+            back[b] = sums(b).astype(jnp.bfloat16)
+            back_copy(b).start()
 
     def fin_copy(to):
         return pltpu.make_async_remote_copy(
@@ -254,9 +255,7 @@
         later[...] = jnp.zeros_like(later)
 
     @pl.loop(0, team)
-    def _(step):
-        slot = peer(step)
-
+    def _(slot):
         @pl.when(has_next)
         def _():
             pltpu.make_async_copy(back.at[slot], later.at[slot], back_recv.at[slot]).wait()
@@ -322,6 +321,10 @@
     width = repeat * HEAD_DIM
     assert key_rows.shape[1] == team * HEAD_DIM
     bf16, f32 = jnp.bfloat16, jnp.float32
+    queries, key_rows, value_rows, out_grad = (
+        pltpu.with_memory_space_constraint(a, pltpu.HBM)
+        for a in (queries, key_rows, value_rows, out_grad)
+    )
     dma = pltpu.SemaphoreType.DMA
     pairs = team * (team + 1) * rows * rows * repeat
     return pl.pallas_call(
@@ -345,8 +348,8 @@
             pltpu.VMEM((team, rows, 2 * HEAD_DIM), bf16),
             pltpu.VMEM((team, rows, 2 * HEAD_DIM), bf16),
             pltpu.VMEM((team + 1, rows, width), f32),
-            pltpu.VMEM(((team + 1) * rows, width), bf16),
-            pltpu.VMEM(((team + 1) * rows, width), bf16),
+            pltpu.VMEM((team, (team + 1) * rows, width), bf16),
+            pltpu.VMEM((team, (team + 1) * rows, width), bf16),
             dma((4, team)), dma((4, team)),
             dma((team,)), dma((team,)),
             dma((2, team)), dma((2, team)),

time: 65 us -> 58.7 us (0.903)
  the two profiles are of different devices: /device:TPU:1 before, /device:TPU:15 now
where the time goes in v2:
time: 58.7 us; the launch traced here: 58.5 us
  Pallas kernels  54.9 us (94%)
  local copies, waits for them, and re-layouts  2.99 us (5%)
  between operations  0.64 us (1%)
    pallas_call x1, Pallas kernels, local(): pl.pallas_call(functools.partial(kernel, team, repeat, tensor_size, total...  54.9 us
    unnamed x4, local copies, waits for them, and re-layouts  2.99 us

profile of v2, /device:TPU:15, one launch (start us, length us, event | category | flops | bytes accessed | tf_op | source)
XLA Modules:
  0.0 58.5 jit_solution(5420238354223660347)
XLA Ops:
  0.6 54.9 %shard_map.75 = (bf16[128,2048]{1,0:T(8,128)(2,1)S(1)}, bf16[128,2048]{1,0:T(8,128)(2,1)S(1)}, bf16[128,1024]{1,0:T(8,128)(2,1)S(1)}, bf16[128,1024]{1,0:T(8,128)(2,1)S(1)}) custom-call(bf16[128,2048]{1,0:T(8,128)(2,1)} %q_hbm.1, bf16[128,1024]{1,0:T(8,128)(2,1)} %k_hbm.1, bf16[128,1024]{1,0:T(8,128)(2,1)} %v_hbm.1, bf16[128,2048]{1,0:T(8,128)(2,1)} %g_hbm.1), custom_call_target="tpu_custom_call" | custom-call | flops 3623878656 | bytes 3145728 | tf_op jit(solution)/shard_map/pallas_call | solution.py:330
  55.6 0.8 %copy.12 = bf16[128,2048]{1,0:T(8,128)(2,1)} copy(bf16[128,2048]{1,0:T(8,128)(2,1)S(1)} %get-tuple-element.8) | data formatting | bytes 1048576
  56.4 0.8 %copy.13 = bf16[128,2048]{1,0:T(8,128)(2,1)} copy(bf16[128,2048]{1,0:T(8,128)(2,1)S(1)} %get-tuple-element.9) | data formatting | bytes 1048576
  57.1 0.7 %copy.14 = bf16[128,1024]{1,0:T(8,128)(2,1)} copy(bf16[128,1024]{1,0:T(8,128)(2,1)S(1)} %get-tuple-element.10) | data formatting | bytes 524288
  57.8 0.7 %copy.15 = bf16[128,1024]{1,0:T(8,128)(2,1)} copy(bf16[128,1024]{1,0:T(8,128)(2,1)S(1)} %get-tuple-element.11) | data formatting | bytes 524288

commit v3 on v2

--- a/solution.py
+++ b/solution.py
@@ -24,9 +24,9 @@
     team, repeat, tensor_size, total,
     q_hbm, k_hbm, v_hbm, g_hbm,
     att_hbm, gq_hbm, gk_hbm, gv_hbm,
-    qb, gb, kv, kvt, dk, dv, att, gq, back, later, fin, land, work, pbuf, dbuf,
+    qb, gb, kv, kvt, dk, dv, att, gq, back, later, fin, work, pbuf, dbuf,
     in_send, in_recv, fwd_send, fwd_recv, out_send, out_recv,
-    back_send, back_recv, fin_send, fin_recv, store_sem,
+    back_send, back_recv, fin_send, fin_recv,
 ):
     rows = q_hbm.shape[0]
     width = repeat * HEAD_DIM
@@ -170,53 +170,65 @@
         def _():
             out_own(kind).start()
 
-    @pl.loop(0, team)
-    def _(step):
-        b = peer(step)
-        in_wait(2, b)
-        in_wait(3, b)
-        q2 = stack(qb[b])
-        g2 = stack(gb[b])
-        q2t = q2.T
-        g2t = g2.T
-        cols = pl.ds(pl.multiple_of(b * rows, rows), span)
-        gone = [jnp.logical_and(jnp.logical_not(has_prev), b + r < team) for r in range(team)]
-        gone.append(None)
-        peak = None
-        for r in range(team + 1):
-            part = contract(kv[b + r, :, :HEAD_DIM], q2t, ((1,), (0,)))
-            if r == 0:
-                part = jnp.where(key_at > query_at, part, masked_score)
-            if r == team:
-                part = jnp.where(key_at <= query_at, part, masked_score)
-            work[r] = part
-            top = jnp.max(part.reshape(rows // 8, 8, width), axis=0)
-            if r < team:
-                top = jnp.where(gone[r], masked_score, top)
-            peak = top if peak is None else jnp.maximum(peak, top)
-        low = jnp.max(peak, axis=0, keepdims=True) * factor
-        denom = None
-        for r in range(team + 1):
-            shift = low if r == team else jnp.where(gone[r], -masked_score, low)
-            expo = jnp.exp2(work[r] * factor - shift)
-            work[r] = expo
-            part = jnp.sum(expo.reshape(rows // 8, 8, width), axis=0)
-            denom = part if denom is None else denom + part
-        inverse = 1.0 / jnp.sum(denom, axis=0, keepdims=True)
-        for r in range(team + 1):
-            probs = work[r] * inverse
-            work[r] = probs
-            pbuf[b, r * rows : (r + 1) * rows] = probs.astype(jnp.bfloat16)
-        out_t = contract(kvt[HEAD_DIM:, cols], pbuf[b], ((1,), (0,)))
-        att[b] = unstack(out_t.T).astype(jnp.bfloat16)
-        ship(0, b)
-        delta = jnp.sum(g2t.astype(jnp.float32) * out_t, axis=0, keepdims=True)
-        for r in range(team + 1):
-            grad_probs = contract(kv[b + r, :, HEAD_DIM:], g2t, ((1,), (0,)))
-            dbuf[b, r * rows : (r + 1) * rows] = (work[r] * (grad_probs - delta)).astype(jnp.bfloat16)
-        dq_t = contract(kvt[:HEAD_DIM, cols], dbuf[b], ((1,), (0,))) * scale
-        gq[b] = unstack(dq_t.T).astype(jnp.bfloat16)
-        ship(1, b)
+    lanes = 4
+
+    @pl.loop(0, team // lanes)
+    def _(turn_at):
+        blocks = [peer(turn_at * lanes + u) for u in range(lanes)]
+        for b in blocks:
+            in_wait(2, b)
+            in_wait(3, b)
+        q2t = [stack(qb[b]).T for b in blocks]
+        g2t = [stack(gb[b]).T for b in blocks]
+        cols = [pl.ds(pl.multiple_of(b * rows, rows), span) for b in blocks]
+        lows = []
+        for u, b in enumerate(blocks):
+            peak = None
+            for r in range(team + 1):
+                part = contract(kv[b + r, :, :HEAD_DIM], q2t[u], ((1,), (0,)))
+                if r == 0:
+                    part = jnp.where(key_at > query_at, part, masked_score)
+                if r == team:
+                    part = jnp.where(key_at <= query_at, part, masked_score)
+                work[u, r] = part
+                top = jnp.max(part.reshape(rows // 8, 8, width), axis=0)
+                if r < team:
+                    gone = jnp.logical_and(jnp.logical_not(has_prev), b + r < team)
+                    top = jnp.where(gone, masked_score, top)
+                peak = top if peak is None else jnp.maximum(peak, top)
+            lows.append(jnp.max(peak, axis=0, keepdims=True) * factor)
+        outs = []
+        for u, b in enumerate(blocks):
+            denom = None
+            for r in range(team + 1):
+                shift = lows[u]
+                if r < team:
+                    gone = jnp.logical_and(jnp.logical_not(has_prev), b + r < team)
+                    shift = jnp.where(gone, -masked_score, shift)
+                expo = jnp.exp2(work[u, r] * factor - shift)
+                work[u, r] = expo
+                part = jnp.sum(expo.reshape(rows // 8, 8, width), axis=0)
+                denom = part if denom is None else denom + part
+            inverse = 1.0 / jnp.sum(denom, axis=0, keepdims=True)
+            for r in range(team + 1):
+                probs = work[u, r] * inverse
+                work[u, r] = probs
+                pbuf[b, r * rows : (r + 1) * rows] = probs.astype(jnp.bfloat16)
+            outs.append(contract(kvt[HEAD_DIM:, cols[u]], pbuf[b], ((1,), (0,))))
+        for u, b in enumerate(blocks):
+            out_t = outs[u]
+            att[b] = unstack(out_t.T).astype(jnp.bfloat16)
+            delta = jnp.sum(g2t[u].astype(jnp.float32) * out_t, axis=0, keepdims=True)
+            for r in range(team + 1):
+                grad_probs = contract(kv[b + r, :, HEAD_DIM:], g2t[u], ((1,), (0,)))
+                dbuf[b, r * rows : (r + 1) * rows] = (
+                    work[u, r] * (grad_probs - delta)
+                ).astype(jnp.bfloat16)
+            dq_t = contract(kvt[:HEAD_DIM, cols[u]], dbuf[b], ((1,), (0,))) * scale
+            gq[b] = unstack(dq_t.T).astype(jnp.bfloat16)
+        for b in blocks:
+            ship(0, b)
+            ship(1, b)
 
     def back_copy(slot):
         return pltpu.make_async_remote_copy(
@@ -240,15 +252,21 @@
             back[b] = sums(b).astype(jnp.bfloat16)
             back_copy(b).start()
 
-    def fin_copy(to):
-        return pltpu.make_async_remote_copy(
-            src_ref=fin.at[to], dst_ref=land.at[member],
-            send_sem=fin_send.at[to], recv_sem=fin_recv.at[member],
+    def fin_refs(kind, slot, source):
+        half, ref = ((k_half, gk_hbm), (v_half, gv_hbm))[kind]
+        return fin.at[slot, :, half], ref.at[:, narrow(source)]
+
+    def fin_copy(kind, to):
+        src, dst = fin_refs(kind, to, member)
+        return pltpu.make_async_remote_copy(
+            src_ref=src, dst_ref=dst,
+            send_sem=fin_send.at[kind, to], recv_sem=fin_recv.at[kind, member],
             device_id=place(base + to), device_id_type=MESH,
         )
 
-    def fin_own():
-        return pltpu.make_async_copy(fin.at[member], land.at[member], fin_recv.at[member])
+    def fin_local(kind, slot):
+        src, dst = fin_refs(kind, slot, slot)
+        return pltpu.make_async_copy(src, dst, fin_recv.at[kind, slot])
 
     @pl.when(jnp.logical_not(has_next))
     def _():
@@ -264,23 +282,13 @@
 
         @pl.when(slot != member)
         def _():
-            fin_copy(slot).start()
+            fin_copy(0, slot).start()
+            fin_copy(1, slot).start()
 
         @pl.when(slot == member)
         def _():
-            fin_own().start()
-
-    for step in range(team):
-        source = lax.rem(member + team - step, team)
-        pltpu.make_async_copy(fin.at[source], land.at[source], fin_recv.at[source]).wait()
-        gk = pltpu.make_async_copy(
-            land.at[source, :, k_half], gk_hbm.at[:, narrow(source)], store_sem.at[0, source]
-        )
-        gv = pltpu.make_async_copy(
-            land.at[source, :, v_half], gv_hbm.at[:, narrow(source)], store_sem.at[1, source]
-        )
-        gk.start()
-        gv.start()
+            fin_local(0, slot).start()
+            fin_local(1, slot).start()
 
     for step in range(team):
         source = peer(step)
@@ -289,19 +297,16 @@
             pltpu.make_async_copy(
                 buf.at[source], ref.at[:, wide(source)], out_recv.at[kind, source]
             ).wait()
-        pltpu.make_async_copy(
-            land.at[source, :, k_half], gk_hbm.at[:, narrow(source)], store_sem.at[0, source]
-        ).wait()
-        pltpu.make_async_copy(
-            land.at[source, :, v_half], gv_hbm.at[:, narrow(source)], store_sem.at[1, source]
-        ).wait()
+        for kind in range(2):
+            fin_local(kind, source).wait()
     for step in range(1, team):
         to = peer(step)
         for kind in range(4):
             in_copy(kind, to).wait_send()
         for kind in range(2):
             out_copy(kind, to).wait_send()
-        fin_copy(to).wait_send()
+        for kind in range(2):
+            fin_copy(kind, to).wait_send()
 
     @pl.when(has_next)
     def _():
@@ -346,16 +351,14 @@
             pltpu.VMEM((team, rows, 2 * HEAD_DIM), bf16),
             pltpu.VMEM((team, rows, 2 * HEAD_DIM), bf16),
             pltpu.VMEM((team, rows, 2 * HEAD_DIM), bf16),
-            pltpu.VMEM((team, rows, 2 * HEAD_DIM), bf16),
-            pltpu.VMEM((team + 1, rows, width), f32),
+            pltpu.VMEM((4, team + 1, rows, width), f32),
             pltpu.VMEM((team, (team + 1) * rows, width), bf16),
             pltpu.VMEM((team, (team + 1) * rows, width), bf16),
             dma((4, team)), dma((4, team)),
             dma((team,)), dma((team,)),
             dma((2, team)), dma((2, team)),
             dma((team,)), dma((team,)),
-            dma((team,)), dma((team,)),
-            dma((2, team)),
+            dma((2, team)), dma((2, team)),
         ],
         compiler_params=pltpu.CompilerParams(
             collective_id=0, has_side_effects=True, vmem_limit_bytes=48 * 1024 * 1024

time: 58.7 us -> 51.7 us (0.88)
  Pallas kernels: 54.9 us -> 47.9 us
    pallas_call x1, Pallas kernels: 54.9 us -> 47.9 us  [local(): pl.pallas_call(functools.partial(kernel, team, repeat, tensor_size, total...]
where the time goes in v3:
time: 51.7 us; the launch traced here: 51.5 us
  Pallas kernels  47.9 us (93%)
  local copies, waits for them, and re-layouts  2.99 us (6%)
  between operations  0.64 us (1%)
    pallas_call x1, Pallas kernels, local(): pl.pallas_call(functools.partial(kernel, team, repeat, tensor_size, total...  47.9 us
    unnamed x4, local copies, waits for them, and re-layouts  2.99 us

profile of v3, /device:TPU:15, one launch (start us, length us, event | category | flops | bytes accessed | tf_op | source)
XLA Modules:
  0.0 51.5 jit_solution(12447494783813247584)
XLA Ops:
  0.6 47.9 %shard_map.75 = (bf16[128,2048]{1,0:T(8,128)(2,1)S(1)}, bf16[128,2048]{1,0:T(8,128)(2,1)S(1)}, bf16[128,1024]{1,0:T(8,128)(2,1)S(1)}, bf16[128,1024]{1,0:T(8,128)(2,1)S(1)}) custom-call(bf16[128,2048]{1,0:T(8,128)(2,1)} %q_hbm.1, bf16[128,1024]{1,0:T(8,128)(2,1)} %k_hbm.1, bf16[128,1024]{1,0:T(8,128)(2,1)} %v_hbm.1, bf16[128,2048]{1,0:T(8,128)(2,1)} %g_hbm.1), custom_call_target="tpu_custom_call" | custom-call | flops 3623878656 | bytes 3145728 | tf_op jit(solution)/shard_map/pallas_call | solution.py:335
  48.5 0.8 %copy.12 = bf16[128,2048]{1,0:T(8,128)(2,1)} copy(bf16[128,2048]{1,0:T(8,128)(2,1)S(1)} %get-tuple-element.8) | data formatting | bytes 1048576
  49.3 0.8 %copy.13 = bf16[128,2048]{1,0:T(8,128)(2,1)} copy(bf16[128,2048]{1,0:T(8,128)(2,1)S(1)} %get-tuple-element.9) | data formatting | bytes 1048576
  50.1 0.7 %copy.14 = bf16[128,1024]{1,0:T(8,128)(2,1)} copy(bf16[128,1024]{1,0:T(8,128)(2,1)S(1)} %get-tuple-element.10) | data formatting | bytes 524288
  50.8 0.7 %copy.15 = bf16[128,1024]{1,0:T(8,128)(2,1)} copy(bf16[128,1024]{1,0:T(8,128)(2,1)S(1)} %get-tuple-element.11) | data formatting | bytes 524288

commit v4 on v3

--- a/solution.py
+++ b/solution.py
@@ -43,6 +43,9 @@
     def peer(step):
         return lax.rem(member + step, team)
 
+    def giver(step):
+        return lax.rem(member + team - step, team)
+
     barrier = pltpu.get_barrier_semaphore()
     for step in range(1, team):
         pl.semaphore_signal(barrier, inc=1, device_id=place(base + peer(step)), device_id_type=MESH)
@@ -105,7 +108,7 @@
         )
 
     for step in range(team):
-        source = peer(step)
+        source = giver(step)
         in_wait(0, source)
         in_wait(1, source)
 
@@ -126,7 +129,7 @@
 
     @pl.loop(0, team)
     def _(step):
-        slot = peer(step)
+        slot = giver(step)
 
         @pl.when(has_prev)
         def _():
@@ -174,7 +177,7 @@
 
     @pl.loop(0, team // lanes)
     def _(turn_at):
-        blocks = [peer(turn_at * lanes + u) for u in range(lanes)]
+        blocks = [giver(turn_at * lanes + u) for u in range(lanes)]
         for b in blocks:
             in_wait(2, b)
             in_wait(3, b)

time: 51.7 us -> 49.2 us (0.952)
  Pallas kernels: 47.9 us -> 45.4 us
    pallas_call x1, Pallas kernels: 47.9 us -> 45.4 us  [local(): pl.pallas_call(functools.partial(kernel, team, repeat, tensor_size, total...]
where the time goes in v4:
time: 49.2 us; the launch traced here: 49.1 us
  Pallas kernels  45.4 us (92%)
  local copies, waits for them, and re-layouts  2.99 us (6%)
  between operations  0.64 us (1%)
    pallas_call x1, Pallas kernels, local(): pl.pallas_call(functools.partial(kernel, team, repeat, tensor_size, total...  45.4 us
    unnamed x4, local copies, waits for them, and re-layouts  2.99 us

profile of v4, /device:TPU:15, one launch (start us, length us, event | category | flops | bytes accessed | tf_op | source)
XLA Modules:
  0.0 49.1 jit_solution(17995281915139474897)
XLA Ops:
  0.6 45.4 %shard_map.75 = (bf16[128,2048]{1,0:T(8,128)(2,1)S(1)}, bf16[128,2048]{1,0:T(8,128)(2,1)S(1)}, bf16[128,1024]{1,0:T(8,128)(2,1)S(1)}, bf16[128,1024]{1,0:T(8,128)(2,1)S(1)}) custom-call(bf16[128,2048]{1,0:T(8,128)(2,1)} %q_hbm.1, bf16[128,1024]{1,0:T(8,128)(2,1)} %k_hbm.1, bf16[128,1024]{1,0:T(8,128)(2,1)} %v_hbm.1, bf16[128,2048]{1,0:T(8,128)(2,1)} %g_hbm.1), custom_call_target="tpu_custom_call" | custom-call | flops 3623878656 | bytes 3145728 | tf_op jit(solution)/shard_map/pallas_call | solution.py:338
  46.1 0.8 %copy.12 = bf16[128,2048]{1,0:T(8,128)(2,1)} copy(bf16[128,2048]{1,0:T(8,128)(2,1)S(1)} %get-tuple-element.8) | data formatting | bytes 1048576
  46.9 0.8 %copy.13 = bf16[128,2048]{1,0:T(8,128)(2,1)} copy(bf16[128,2048]{1,0:T(8,128)(2,1)S(1)} %get-tuple-element.9) | data formatting | bytes 1048576
  47.7 0.7 %copy.14 = bf16[128,1024]{1,0:T(8,128)(2,1)} copy(bf16[128,1024]{1,0:T(8,128)(2,1)S(1)} %get-tuple-element.10) | data formatting | bytes 524288
  48.4 0.7 %copy.15 = bf16[128,1024]{1,0:T(8,128)(2,1)} copy(bf16[128,1024]{1,0:T(8,128)(2,1)S(1)} %get-tuple-element.11) | data formatting | bytes 524288
